TPU v7x, 32 devices: a whole 2x2x4 slice. The times are simulated.
32 devices in a mesh: tm: 4 (over y, core), space: 8 (over z, x).
Axes of the slice: x: 2, y: 2, z: 4, core: 2. Of those that a mesh axis runs over, the one named last changes fastest.
Arguments:
- initial: float32 [4, 3, 8, 16, 16, 128], P('tm', None, 'space'), may hold values from -3 to 3
Outputs:
- end_state: float32 [4, 3, 8, 16, 16, 128], P('tm', None, 'space')
All inputs are finite; a program needn't handle non-finite values.
Results may differ from a plain program's by a relative error of at most 0.0001.
Values sent between devices are 32-bit elements; how exact they have to be, the bound alone decides.
A program may use at most 128 MiB of HBM per device.

v0:
```python
import functools
import jax
import jax.numpy as jnp
import numpy as np
from jax import lax
from jax.experimental import pallas as pl
from jax.experimental.pallas import tpu as pltpu
from jax.sharding import PartitionSpec as P

YBRICKS = 4
FINE = 16
COARSE = 8
LANES = 128
TIME_STEP = 0.001
VISCOSITY = 0.05
QUAD_WEIGHTS = ((5.0 / 24.0, 1.0 / 3.0, -1.0 / 24.0), (-1.0 / 24.0, 1.0 / 3.0, 5.0 / 24.0))
MESH = pl.DeviceIdType.MESH
F32 = jnp.float32
BF16 = jnp.bfloat16


def cheb_tables(count):
    index = np.arange(count)
    points = -np.cos(np.pi * index / (count - 1))
    weights = (-1.0) ** index
    weights[0] = weights[0] * 0.5
    weights[-1] = weights[-1] * 0.5
    return (points, weights)


def diff_matrix(points, weights):
    count = points.shape[0]
    ident = np.eye(count)
    gaps = points[:, None] - points[None, :] + ident
    matrix = weights[None, :] / weights[:, None] / gaps
    matrix = matrix * (1.0 - ident)
    return matrix - ident * matrix.sum(axis=1)[:, None]


def interp_matrix(points, weights, targets):
    gaps = targets[:, None] - points[None, :]
    exact_hit = np.abs(gaps) < 1e-12
    safe_gaps = np.where(exact_hit, 1.0, gaps)
    terms = weights[None, :] / safe_gaps
    matrix = terms / terms.sum(axis=1, keepdims=True)
    any_hit = exact_hit.any(axis=1)
    return np.where(any_hit[:, None], np.where(exact_hit, 1.0, 0.0), matrix)


def lifted_matrix(count, length, periodic):
    points, weights = cheb_tables(count)
    matrix = np.kron(np.eye(length // count), diff_matrix(points, weights))
    lift_coef = (count - 1) ** 2 / 2.0
    for place in range(length):
        if place % count == 0:
            matrix[place, place] += lift_coef
            if place > 0:
                matrix[place, place - 1] -= lift_coef
            elif periodic:
                matrix[place, length - 1] -= lift_coef
        if place % count == count - 1:
            matrix[place, place] -= lift_coef
            if place < length - 1:
                matrix[place, place + 1] += lift_coef
            elif periodic:
                matrix[place, 0] += lift_coef
    return matrix


def halves(matrix):
    high = np.asarray(matrix, np.float32).astype(jnp.bfloat16)
    low = (np.asarray(matrix, np.float64) - high.astype(np.float64)).astype(np.float32).astype(jnp.bfloat16)
    return high, low


def left_table(matrix):
    high, low = halves(matrix)
    return np.concatenate([high, high, low], axis=1)


def right_table(matrix):
    high, low = halves(matrix)
    return np.concatenate([high, high, low], axis=0)


def padded(matrix, rows, columns):
    return np.pad(matrix, ((0, rows - matrix.shape[0]), (0, columns - matrix.shape[1])))


def level_tables(count, side, z_length, lanes):
    brick = lifted_matrix(count, side, False)
    lift = (count - 1) ** 2 / 2.0
    ident = np.eye(side)
    first, last = ident[:, :1], ident[:, -1:]
    second = brick @ brick - lift**2 * (first @ first.T + last @ last.T)
    along_x = lambda m: np.kron(m, ident)
    along_y = lambda m: np.kron(ident, m)
    inner = np.concatenate(
        [along_x(brick), along_y(brick), VISCOSITY * (along_x(second) + along_y(second))]
    )
    faces = np.concatenate(
        [form(m) for form in (along_x, along_y) for e in (first, last) for m in (e.T, e.T @ brick)]
    )
    grad_cols, visc_cols = [], []
    for e, sign in ((first, -lift), (last, lift)):
        grad_cols += [sign * e, 0.0 * e]
        visc_cols += [VISCOSITY * sign * (brick @ e), VISCOSITY * sign * e]
    nothing = [0.0 * first] * 4
    rows = lambda cx, cy: np.concatenate([along_x(m) for m in cx] + [along_y(m) for m in cy], axis=1)
    outer = np.concatenate(
        [rows(grad_cols, nothing), rows(nothing, grad_cols), rows(visc_cols, visc_cols)]
    )
    depth = lifted_matrix(count, z_length, True)
    depth_t = np.concatenate(
        [padded(depth.T, lanes, lanes), padded(VISCOSITY * (depth @ depth).T, lanes, lanes)], axis=1
    )
    return [left_table(inner), left_table(faces), left_table(outer), right_table(depth_t)]


def split(value):
    high = value.astype(BF16)
    low = (value - high.astype(F32)).astype(BF16)
    return high, low


def stacked(value):
    high, low = split(value)
    return jnp.concatenate([high, low, high], axis=0)


def left(table, value3):
    return jnp.dot(table[...], value3, preferred_element_type=F32)


def right(value, table, lanes):
    high, low = split(value)
    blocks = []
    for at in range(0, value.shape[1], lanes):
        h, l = high[:, at : at + lanes], low[:, at : at + lanes]
        blocks.append(jnp.concatenate([h, l, h], axis=1))
    return jnp.dot(jnp.concatenate(blocks, axis=0), table[...], preferred_element_type=F32)


def unstack(value, rows):
    return jnp.concatenate([value[at : at + rows] for at in range(0, value.shape[0], rows)], axis=1)


def kernel(geometry, q_ref, *refs):
    slices, bricks, fine_rows, coarse_rows, lanes = geometry
    tables, refs = refs[:12], refs[12:]
    fine_tab, coarse_tab = tables[:4], tables[4:8]
    restrict_rows, restrict_z, prolong_rows, prolong_z = tables[8:]
    out_ref, refs = refs[0], refs[1:]
    (v1, v2, start, rates, nodes, f_send, f_recv, f_acc, c_send, c_recv, c_acc, seq, terms, saved,
     f_ssem, f_rsem, c_ssem, c_rsem, t_ssem, t_rsem, s_ssem, s_rsem) = refs

    p = lax.axis_index("tm")
    b = lax.axis_index("space")
    column = lax.rem(b, YBRICKS)
    base = b - column
    x_low = lax.rem(b + bricks - YBRICKS, bricks)
    x_high = lax.rem(b + YBRICKS, bricks)
    y_low = base + lax.rem(column + YBRICKS - 1, YBRICKS)
    y_high = base + lax.rem(column + 1, YBRICKS)
    targets = (x_low, x_high, y_low, y_high)
    landing = (1, 0, 3, 2)

    barrier = pltpu.get_barrier_semaphore()
    for target in targets:
        pl.semaphore_signal(barrier, inc=1, device_id={"space": target}, device_id_type=MESH)
    for k in range(1, slices):
        pl.semaphore_signal(
            barrier, inc=1, device_id={"tm": lax.rem(p + k, slices)}, device_id_type=MESH
        )
    pl.semaphore_wait(barrier, 4 + slices - 1)

    def copies(send, recv, ssem, rsem, slot):
        size = send.shape[1] // 4
        return [
            pltpu.make_async_remote_copy(
                src_ref=send.at[slot, pl.ds(d * size, size)],
                dst_ref=recv.at[slot, pl.ds(landing[d] * size, size)],
                send_sem=ssem.at[slot, d],
                recv_sem=rsem.at[slot, landing[d]],
                device_id={"space": targets[d]},
                device_id_type=MESH,
            )
            for d in range(4)
        ]

    fine_part = (f_send, f_recv, f_ssem, f_rsem)
    coarse_part = (c_send, c_recv, c_ssem, c_rsem)

    def begin(value, tab, part, slot):
        value3 = stacked(value)
        part[0][slot] = left(tab[1], value3)
        for copy in copies(*part, slot):
            copy.start()
        return value3

    def local(value, value3, tab, acc):
        rows = value.shape[0]
        acc[:, : 3 * lanes] = left(tab[0], value3)
        deep = right(value, tab[3], lanes)
        for c in range(3):
            at = slice(c * lanes, (c + 1) * lanes)
            one = deep[c * rows : (c + 1) * rows]
            acc[:rows, 3 * lanes + c * lanes : 4 * lanes + c * lanes] = one[:, :lanes]
            acc[2 * rows :, at] += one[:, lanes:]

    def finish(value, tab, part, slot, acc):
        rows = value.shape[0]
        for copy in copies(*part, slot):
            copy.wait()
        total = acc[:, : 3 * lanes] + left(tab[2], stacked(part[1][slot]))
        out = []
        for c in range(3):
            at = slice(c * lanes, (c + 1) * lanes)
            deep = acc[:rows, 3 * lanes + c * lanes : 4 * lanes + c * lanes]
            out.append(
                total[2 * rows :, at]
                - (
                    value[:, :lanes] * total[:rows, at]
                    + value[:, lanes : 2 * lanes] * total[rows : 2 * rows, at]
                    + value[:, 2 * lanes :] * deep
                )
            )
        return jnp.concatenate(out, axis=1)

    def restrict(value):
        less = left(restrict_rows, stacked(value))
        return unstack(right(less, restrict_z, lanes), coarse_rows)

    def prolong(value):
        deep = unstack(right(value, prolong_z, lanes), coarse_rows)
        return left(prolong_rows, stacked(deep))

    h = TIME_STEP
    q = jnp.concatenate([q_ref[c] for c in range(3)], axis=1)
    q3 = begin(q, fine_tab, fine_part, 0)
    local(q, q3, fine_tab, f_acc)
    saved[0] = restrict(q)
    seq[0] = saved[0]
    rates[0] = finish(q, fine_tab, fine_part, 0, f_acc)

    v1[...] = q + (0.5 * h) * rates[0]
    w3 = begin(v1[...], fine_tab, fine_part, 1)
    saved[1] = restrict(v1[...])
    c0 = begin(saved[0], coarse_tab, coarse_part, 0)
    c1 = begin(saved[1], coarse_tab, coarse_part, 1)
    local(v1[...], w3, fine_tab, f_acc)
    rates[1] = finish(v1[...], fine_tab, fine_part, 1, f_acc)
    v2[...] = v1[...] + (0.5 * h) * rates[1]
    w3 = begin(v2[...], fine_tab, fine_part, 2)

    def hand_on():
        return pltpu.make_async_remote_copy(
            src_ref=v2,
            dst_ref=start,
            send_sem=s_ssem,
            recv_sem=s_rsem,
            device_id={"tm": lax.rem(p + 1, slices)},
            device_id_type=MESH,
        )

    @pl.when(p + 1 < slices)
    def _():
        hand_on().start()

    @pl.when(p == 0)
    def _():
        for c in range(3):
            start[:, c * lanes : (c + 1) * lanes] = q_ref[c]

    local(v2[...], w3, fine_tab, f_acc)
    for m, value3 in ((0, c0), (1, c1)):
        local(saved[m], value3, coarse_tab, c_acc)
        saved[3 + m] = finish(saved[m], coarse_tab, coarse_part, m, c_acc)
    saved[2] = restrict(v2[...])
    known = [restrict(rates[0]), restrict(rates[1])]
    known.append(restrict(finish(v2[...], fine_tab, fine_part, 2, f_acc)))
    for m in range(2):
        row = QUAD_WEIGHTS[m]
        mixed = h * (row[0] * known[0] + row[1] * known[1] + row[2] * known[2])
        if m == 0:
            terms[2 * p] = mixed + jnp.where(p == 0, saved[0], (-0.5 * h) * saved[3])
        else:
            terms[2 * p + 1] = mixed - (0.5 * h) * saved[4]

    def term_copy(source, k):
        return pltpu.make_async_remote_copy(
            src_ref=terms.at[pl.ds(2 * source, 2)],
            dst_ref=terms.at[pl.ds(2 * source, 2)],
            send_sem=t_ssem.at[k],
            recv_sem=t_rsem.at[source],
            device_id={"tm": lax.rem(p + k, slices)},
            device_id_type=MESH,
        )

    for k in range(slices - 1, 0, -1):
        @pl.when(p + k < slices)
        def _():
            term_copy(p, k).start()

    @pl.when(p > 0)
    def _():
        hand_on().wait_recv()

    saved[5] = restrict(start[...])

    @pl.when(p > 0)
    def _():
        term_copy(0, 1).wait_recv()

    seq[1] = terms[0]

    def stage(r, carry):
        value = seq[r + 1]
        value3 = begin(value, coarse_tab, coarse_part, r + 2)
        local(value, value3, coarse_tab, c_acc)
        source = (r + 1) // 2

        @pl.when((r % 2 == 1) & (source < p))
        def _():
            term_copy(source, 1).wait_recv()

        rate = finish(value, coarse_tab, coarse_part, r + 2, c_acc)
        seq[r + 2] = value + (0.5 * h) * rate + terms[r + 1]
        return carry

    lax.fori_loop(0, 2 * p + 1, stage, 0)

    for k in range(1, slices):
        @pl.when(p + k < slices)
        def _():
            term_copy(p, k).wait_send()

    @pl.when(p + 1 < slices)
    def _():
        hand_on().wait_send()

    values3 = []
    for m, (whole, part) in enumerate(((start, saved.at[5]), (v1, saved.at[1]), (v2, saved.at[2]))):
        nodes[m] = whole[...] + prolong(seq[2 * p + m] - part[...])
        values3.append(begin(nodes[m], fine_tab, fine_part, 3 + m))
    for m in range(3):
        local(nodes[m], values3[m], fine_tab, f_acc)
        rates[m] = finish(nodes[m], fine_tab, fine_part, 3 + m, f_acc)

    row = QUAD_WEIGHTS[0]
    v1[...] = nodes[0] + h * (row[0] * rates[0] + row[1] * rates[1] + row[2] * rates[2])
    w3 = begin(v1[...], fine_tab, fine_part, 6)
    local(v1[...], w3, fine_tab, f_acc)
    row = QUAD_WEIGHTS[1]
    v2[...] = v1[...] + h * (row[0] * rates[0] + (row[1] - 0.5) * rates[1] + row[2] * rates[2])
    last = v2[...] + (0.5 * h) * finish(v1[...], fine_tab, fine_part, 6, f_acc)
    for c in range(3):
        out_ref[c] = last[:, c * lanes : (c + 1) * lanes]


def solution(mesh):
    slices, bricks = mesh.shape["tm"], mesh.shape["space"]

    def shards(initial):
        side, z_length = initial.shape[3], initial.shape[-1]
        lanes = z_length
        half = side // 2
        fine_rows, coarse_rows = side * side, half * half
        fine_points, fine_weights = cheb_tables(FINE)
        coarse_points, coarse_weights = cheb_tables(COARSE)
        down = interp_matrix(fine_points, fine_weights, coarse_points)
        up = interp_matrix(coarse_points, coarse_weights, fine_points)
        spread = lambda m, length: np.kron(np.eye(length // m.shape[1]), m)
        down_side, up_side = spread(down, side), spread(up, half)
        tables = (
            level_tables(FINE, side, z_length, lanes)
            + level_tables(COARSE, half, z_length // 2, lanes)
            + [
                left_table(np.kron(down_side, down_side)),
                right_table(padded(spread(down, z_length).T, lanes, lanes)),
                left_table(np.kron(up_side, up_side)),
                right_table(padded(spread(up, z_length // 2).T, lanes, lanes)),
            ]
        )
        wide = 3 * lanes
        fine_slots, coarse_slots = 7, 2 * slices + 1
        fine_field = pltpu.VMEM((fine_rows, wide), F32)
        geometry = (slices, bricks, fine_rows, coarse_rows, lanes)
        result = pl.pallas_call(
            functools.partial(kernel, geometry),
            out_shape=jax.ShapeDtypeStruct((3, fine_rows, lanes), F32),
            in_specs=[pl.BlockSpec(memory_space=pltpu.VMEM)] * (1 + len(tables)),
            out_specs=pl.BlockSpec(memory_space=pltpu.VMEM),
            scratch_shapes=[
                fine_field,
                fine_field,
                fine_field,
                pltpu.VMEM((3, fine_rows, wide), F32),
                pltpu.VMEM((3, fine_rows, wide), F32),
                pltpu.VMEM((fine_slots, 8 * side, wide), F32),
                pltpu.VMEM((fine_slots, 8 * side, wide), F32),
                pltpu.VMEM((3 * fine_rows, 2 * wide), F32),
                pltpu.VMEM((coarse_slots, 8 * half, wide), F32),
                pltpu.VMEM((coarse_slots, 8 * half, wide), F32),
                pltpu.VMEM((3 * coarse_rows, 2 * wide), F32),
                pltpu.VMEM((2 * slices + 1, coarse_rows, wide), F32),
                pltpu.VMEM((2 * slices, coarse_rows, wide), F32),
                pltpu.VMEM((6, coarse_rows, wide), F32),
                pltpu.SemaphoreType.DMA((fine_slots, 4)),
                pltpu.SemaphoreType.DMA((fine_slots, 4)),
                pltpu.SemaphoreType.DMA((coarse_slots, 4)),
                pltpu.SemaphoreType.DMA((coarse_slots, 4)),
                pltpu.SemaphoreType.DMA((slices,)),
                pltpu.SemaphoreType.DMA((slices,)),
                pltpu.SemaphoreType.DMA,
                pltpu.SemaphoreType.DMA,
            ],
            compiler_params=pltpu.CompilerParams(
                collective_id=0, has_side_effects=True, vmem_limit_bytes=40 * 2**20
            ),
        )(initial.reshape(3, fine_rows, lanes), *[jnp.asarray(t) for t in tables])
        return result.reshape(initial.shape)

    return jax.shard_map(
        shards,
        mesh=mesh,
        in_specs=(P("tm", None, "space", None, None, None),),
        out_specs=P("tm", None, "space", None, None, None),
        check_vma=False,
    )
```

profile of v0, /device:TPU:5, one launch (start us, length us, event | category | flops | bytes accessed | tf_op | source)
XLA Modules:
  0.0 91.8 jit_solution(15515050485611628770)
XLA Ops:
  0.0 0.0 copy-start
  0.0 1.3 %copy-done = bf16[768,768]{1,0:T(8,128)(2,1)S(1)} copy-done((bf16[768,768]{1,0:T(8,128)(2,1)S(1)}, bf16[768,768]{1,0:T(8,128)(2,1)}, u32[]{:S(2)}) %copy-start) | copy-done | bytes 1179672
  1.3 0.0 copy-start.1
  1.3 1.1 %copy-done.1 = bf16[768,384]{1,0:T(8,128)(2,1)S(1)} copy-done((bf16[768,384]{1,0:T(8,128)(2,1)S(1)}, bf16[768,384]{1,0:T(8,128)(2,1)}, u32[]{:S(2)}) %copy-start.1) | copy-done | bytes 589848
  2.3 0.0 copy-start.2
  2.3 1.0 %copy-done.2 = f32[1,3,1,16,16,128]{5,4,3,2,1,0:T(8,128)S(1)} copy-done((f32[1,3,1,16,16,128]{5,4,3,2,1,0:T(8,128)S(1)}, f32[1,3,1,16,16,128]{5,4,3,2,1,0:T(8,128)}, u32[]{:S(2)}) %copy-start.2) | copy-done | bytes 393240
  3.3 0.0 copy-start.3
  3.3 0.9 %copy-done.3 = bf16[384,256]{1,0:T(8,128)(2,1)S(1)} copy-done((bf16[384,256]{1,0:T(8,128)(2,1)S(1)}, bf16[384,256]{1,0:T(8,128)(2,1)}, u32[]{:S(2)}) %copy-start.3) | copy-done | bytes 196632
  4.3 0.0 copy-start.4
  4.3 0.9 %copy-done.4 = bf16[384,256]{1,0:T(8,128)(2,1)S(1)} copy-done((bf16[384,256]{1,0:T(8,128)(2,1)S(1)}, bf16[384,256]{1,0:T(8,128)(2,1)}, u32[]{:S(2)}) %copy-start.4) | copy-done | bytes 196632
  5.2 0.0 copy-start.5
  5.2 0.9 %copy-done.5 = bf16[128,768]{1,0:T(8,128)(2,1)S(1)} copy-done((bf16[128,768]{1,0:T(8,128)(2,1)S(1)}, bf16[128,768]{1,0:T(8,128)(2,1)}, u32[]{:S(2)}) %copy-start.5) | copy-done | bytes 196632
  6.1 0.0 copy-start.6
  6.1 0.9 copy-done.6
  7.0 0.0 copy-start.7
  7.0 0.9 copy-done.7
  7.9 0.0 copy-start.8
  7.9 0.9 copy-done.8
  8.8 0.0 copy-start.9
  8.8 0.9 copy-done.9
  9.7 0.0 copy-start.10
  9.7 0.9 copy-done.10
  10.6 0.0 copy-start.11
  10.6 0.9 copy-done.11
  11.5 0.0 copy-start.12
  11.5 0.8 copy-done.12
  12.2 78.8 %shard_map.127 = f32[3,256,128]{2,1,0:T(8,128)S(1)} custom-call(f32[3,256,128]{2,1,0:T(8,128)S(1)} %bitcast.5, bf16[768,768]{1,0:T(8,128)(2,1)S(1)} %copy-done, bf16[128,768]{1,0:T(8,128)(2,1)S(1)} %copy-done.5, bf16[768,384]{1,0:T(8,128)(2,1)S(1)} %copy-done.1, bf16[384,256]{1,0:T(8,128)(2,1)S(1)} %copy-done.4, bf16[192,192]{1,0:T(8,128)(2,1)S(1)} %copy-done.11, ...), custom_call_target="tpu_custom_call" | custom-call | tf_op jit(solution)/shard_map/pallas_call | solution.py:389
  91.1 0.7 copy.16
Async XLA Ops:
  0.0 1.3 %copy-start = (bf16[768,768]{1,0:T(8,128)(2,1)S(1)}, bf16[768,768]{1,0:T(8,128)(2,1)}, u32[]{:S(2)}) copy-start(bf16[768,768]{1,0:T(8,128)(2,1)} %constant.24.clone.refs_0_) | copy-start | bytes 3538948
  1.3 1.1 %copy-start.1 = (bf16[768,384]{1,0:T(8,128)(2,1)S(1)}, bf16[768,384]{1,0:T(8,128)(2,1)}, u32[]{:S(2)}) copy-start(bf16[768,384]{1,0:T(8,128)(2,1)} %constant.26.clone.refs_2_) | copy-start | bytes 1769476
  2.3 1.0 %copy-start.2 = (f32[1,3,1,16,16,128]{5,4,3,2,1,0:T(8,128)S(1)}, f32[1,3,1,16,16,128]{5,4,3,2,1,0:T(8,128)}, u32[]{:S(2)}) copy-start(f32[1,3,1,16,16,128]{5,4,3,2,1,0:T(8,128)} %param.13) | copy-start | bytes 1179652
  3.3 0.9 %copy-start.3 = (bf16[384,256]{1,0:T(8,128)(2,1)S(1)}, bf16[384,256]{1,0:T(8,128)(2,1)}, u32[]{:S(2)}) copy-start(bf16[384,256]{1,0:T(8,128)(2,1)} %constant.31.clone.refs_7_) | copy-start | bytes 589828
  4.3 0.9 %copy-start.4 = (bf16[384,256]{1,0:T(8,128)(2,1)S(1)}, bf16[384,256]{1,0:T(8,128)(2,1)}, u32[]{:S(2)}) copy-start(bf16[384,256]{1,0:T(8,128)(2,1)} %constant.27.clone.refs_3_) | copy-start | bytes 589828
  5.2 0.9 %copy-start.5 = (bf16[128,768]{1,0:T(8,128)(2,1)S(1)}, bf16[128,768]{1,0:T(8,128)(2,1)}, u32[]{:S(2)}) copy-start(bf16[128,768]{1,0:T(8,128)(2,1)} %constant.25.clone.refs_1_) | copy-start | bytes 589828
  6.1 0.9 copy-start.6
  7.0 0.9 copy-start.7
  7.9 0.9 copy-start.8
  8.8 0.9 copy-start.9
  9.7 0.9 copy-start.10
  10.6 0.9 copy-start.11
  11.5 0.8 copy-start.12
where the time goes:
time: 93.5 us; the launch traced here: 91.8 us
  Pallas kernels  78.8 us (84%)
  local copies, waits for them, and re-layouts  13 us (14%)
    pallas_call x1, Pallas kernels, shards(): pl.pallas_call(functools.partial(kernel, geometry), out_shape=jax.ShapeDt...  78.8 us
    unnamed x27, local copies, waits for them, and re-layouts  13 us

commit v1 on v0

--- a/solution.py
+++ b/solution.py
@@ -87,7 +87,18 @@
     return np.pad(matrix, ((0, rows - matrix.shape[0]), (0, columns - matrix.shape[1])))
 
 
-def level_tables(count, side, z_length, lanes):
+def face_rows(brick, side, packed):
+    ident = np.eye(side)
+    ends = (ident[:1], ident[-1:])
+    forms = (lambda m: np.kron(m, ident), lambda m: np.kron(ident, m))
+    value = [form(e) for form in forms for e in ends]
+    slope = [form(e @ brick) for form in forms for e in ends]
+    if packed:
+        return value + slope
+    return [m for pair in zip(value, slope) for m in pair]
+
+
+def level_tables(count, side, z_length, lanes, packed):
     brick = lifted_matrix(count, side, False)
     lift = (count - 1) ** 2 / 2.0
     ident = np.eye(side)
@@ -98,22 +109,27 @@
     inner = np.concatenate(
         [along_x(brick), along_y(brick), VISCOSITY * (along_x(second) + along_y(second))]
     )
-    faces = np.concatenate(
-        [form(m) for form in (along_x, along_y) for e in (first, last) for m in (e.T, e.T @ brick)]
-    )
+    faces = np.concatenate(face_rows(brick, side, packed))
     grad_cols, visc_cols = [], []
     for e, sign in ((first, -lift), (last, lift)):
         grad_cols += [sign * e, 0.0 * e]
         visc_cols += [VISCOSITY * sign * (brick @ e), VISCOSITY * sign * e]
     nothing = [0.0 * first] * 4
-    rows = lambda cx, cy: np.concatenate([along_x(m) for m in cx] + [along_y(m) for m in cy], axis=1)
+    order = [0, 2, 4, 6, 1, 3, 5, 7] if packed else list(range(8))
+
+    def rows(cx, cy):
+        columns = [along_x(m) for m in cx] + [along_y(m) for m in cy]
+        return np.concatenate([columns[i] for i in order], axis=1)
+
     outer = np.concatenate(
         [rows(grad_cols, nothing), rows(nothing, grad_cols), rows(visc_cols, visc_cols)]
     )
     depth = lifted_matrix(count, z_length, True)
+    twice = lanes // z_length
     depth_t = np.concatenate(
-        [padded(depth.T, lanes, lanes), padded(VISCOSITY * (depth @ depth).T, lanes, lanes)], axis=1
+        [np.tile(m.T, (1, twice)) for m in (depth, VISCOSITY * (depth @ depth))], axis=1
     )
+    depth_t = padded(depth_t, lanes, 2 * lanes)
     return [left_table(inner), left_table(faces), left_table(outer), right_table(depth_t)]
 
 
@@ -145,14 +161,25 @@
     return jnp.concatenate([value[at : at + rows] for at in range(0, value.shape[0], rows)], axis=1)
 
 
-def kernel(geometry, q_ref, *refs):
+def kernel(geometry, table_count, q_hbm, *refs):
     slices, bricks, fine_rows, coarse_rows, lanes = geometry
-    tables, refs = refs[:12], refs[12:]
+    sources, refs = refs[:table_count], refs[table_count:]
+    out_ref, q_ref, refs = refs[0], refs[1], refs[2:]
+    tables, refs = refs[:table_count], refs[table_count:]
     fine_tab, coarse_tab = tables[:4], tables[4:8]
-    restrict_rows, restrict_z, prolong_rows, prolong_z = tables[8:]
-    out_ref, refs = refs[0], refs[1:]
-    (v1, v2, start, rates, nodes, f_send, f_recv, f_acc, c_send, c_recv, c_acc, seq, terms, saved,
-     f_ssem, f_rsem, c_ssem, c_rsem, t_ssem, t_rsem, s_ssem, s_rsem) = refs
+    (restrict_rows, restrict_z, prolong_rows, prolong_z,
+     delta_faces, halo_z, halo_rows) = tables[8:]
+    (l_sem, v1, v2, start, start_halo, rates, nodes, f_send, f_recv, f_acc, c_send, c_recv, c_acc,
+     seq, terms, saved, f_ssem, f_rsem, c_ssem, c_rsem, t_ssem, t_rsem, s_ssem, s_rsem) = refs
+    half = lanes // 2
+    size = c_send.shape[1]
+
+    q_load = pltpu.make_async_copy(q_hbm, q_ref, l_sem.at[table_count])
+    q_load.start()
+    loads = {}
+    for i in (1, 0, 3, 2, 8, 9, 5, 4, 7, 6, 10, 11, 12, 13, 14):
+        loads[i] = pltpu.make_async_copy(sources[i], tables[i], l_sem.at[i])
+        loads[i].start()
 
     p = lax.axis_index("tm")
     b = lax.axis_index("space")
@@ -190,13 +217,23 @@
 
     fine_part = (f_send, f_recv, f_ssem, f_rsem)
     coarse_part = (c_send, c_recv, c_ssem, c_rsem)
-
-    def begin(value, tab, part, slot):
-        value3 = stacked(value)
-        part[0][slot] = left(tab[1], value3)
+    low_lanes = lax.broadcasted_iota(jnp.int32, (size, 3 * lanes), 1) % lanes < half
+
+    def begin(value3, slot):
+        f_send[slot] = left(fine_tab[1], value3)
+        for copy in copies(*fine_part, slot):
+            copy.start()
+
+    def coarse_begin(value3, table, slot):
+        faces = left(table, value3)
+        c_send[slot] = jnp.where(low_lanes, faces[:size], faces[size:])
+        for copy in copies(*coarse_part, slot):
+            copy.start()
+
+    def arrive(part, slot):
         for copy in copies(*part, slot):
-            copy.start()
-        return value3
+            copy.wait()
+        return part[1][slot]
 
     def local(value, value3, tab, acc):
         rows = value.shape[0]
@@ -208,11 +245,9 @@
             acc[:rows, 3 * lanes + c * lanes : 4 * lanes + c * lanes] = one[:, :lanes]
             acc[2 * rows :, at] += one[:, lanes:]
 
-    def finish(value, tab, part, slot, acc):
+    def finish(value, tab, halo, acc):
         rows = value.shape[0]
-        for copy in copies(*part, slot):
-            copy.wait()
-        total = acc[:, : 3 * lanes] + left(tab[2], stacked(part[1][slot]))
+        total = acc[:, : 3 * lanes] + left(tab[2], stacked(halo))
         out = []
         for c in range(3):
             at = slice(c * lanes, (c + 1) * lanes)
@@ -227,58 +262,87 @@
             )
         return jnp.concatenate(out, axis=1)
 
-    def restrict(value):
-        less = left(restrict_rows, stacked(value))
-        return unstack(right(less, restrict_z, lanes), coarse_rows)
+    def coarse_finish(value, slot, acc):
+        got = arrive(coarse_part, slot)
+        turned = jnp.concatenate(
+            [pltpu.roll(got[:, c * lanes : (c + 1) * lanes], half, 1) for c in range(3)], axis=1
+        )
+        halo = jnp.concatenate(
+            [jnp.where(low_lanes, got, turned), jnp.where(low_lanes, turned, got)], axis=0
+        )
+        return finish(value, coarse_tab, halo, acc)
+
+    def restrict(value3):
+        return unstack(right(left(restrict_rows, value3), restrict_z, lanes), coarse_rows)
 
     def prolong(value):
         deep = unstack(right(value, prolong_z, lanes), coarse_rows)
         return left(prolong_rows, stacked(deep))
 
+    def prolong_halo(got):
+        both = right(got, halo_z, lanes)
+        parts = [unstack(both[:, :lanes], size), unstack(both[:, lanes:], size)]
+        return left(halo_rows, stacked(jnp.concatenate(parts, axis=0)))
+
     h = TIME_STEP
+    q_load.wait()
     q = jnp.concatenate([q_ref[c] for c in range(3)], axis=1)
-    q3 = begin(q, fine_tab, fine_part, 0)
-    local(q, q3, fine_tab, f_acc)
-    saved[0] = restrict(q)
+    value3 = stacked(q)
+    loads[1].wait()
+    begin(value3, 0)
+    for i in (0, 3):
+        loads[i].wait()
+    local(q, value3, fine_tab, f_acc.at[0])
+    for i in (2, 8, 9):
+        loads[i].wait()
+    saved[0] = restrict(value3)
     seq[0] = saved[0]
-    rates[0] = finish(q, fine_tab, fine_part, 0, f_acc)
+    rates[0] = finish(q, fine_tab, arrive(fine_part, 0), f_acc.at[0])
 
     v1[...] = q + (0.5 * h) * rates[0]
-    w3 = begin(v1[...], fine_tab, fine_part, 1)
-    saved[1] = restrict(v1[...])
-    c0 = begin(saved[0], coarse_tab, coarse_part, 0)
-    c1 = begin(saved[1], coarse_tab, coarse_part, 1)
-    local(v1[...], w3, fine_tab, f_acc)
-    rates[1] = finish(v1[...], fine_tab, fine_part, 1, f_acc)
+    value3 = stacked(v1[...])
+    begin(value3, 1)
+    saved[1] = restrict(value3)
+    for i in (4, 5, 6, 7, 10, 11, 12, 13, 14):
+        loads[i].wait()
+    for m in range(2):
+        coarse3 = stacked(saved[m])
+        coarse_begin(coarse3, coarse_tab[1], m)
+        local(saved[m], coarse3, coarse_tab, c_acc.at[m])
+    local(v1[...], value3, fine_tab, f_acc.at[0])
+    rates[1] = finish(v1[...], fine_tab, arrive(fine_part, 1), f_acc.at[0])
     v2[...] = v1[...] + (0.5 * h) * rates[1]
-    w3 = begin(v2[...], fine_tab, fine_part, 2)
-
-    def hand_on():
+    value3 = stacked(v2[...])
+    begin(value3, 2)
+
+    def hand_on(source, target, which):
         return pltpu.make_async_remote_copy(
-            src_ref=v2,
-            dst_ref=start,
-            send_sem=s_ssem,
-            recv_sem=s_rsem,
+            src_ref=source,
+            dst_ref=target,
+            send_sem=s_ssem.at[which],
+            recv_sem=s_rsem.at[which],
             device_id={"tm": lax.rem(p + 1, slices)},
             device_id_type=MESH,
         )
 
+    handed = lambda: (hand_on(v2, start, 0), hand_on(f_recv.at[2], start_halo, 1))
+
     @pl.when(p + 1 < slices)
     def _():
-        hand_on().start()
+        handed()[0].start()
 
     @pl.when(p == 0)
     def _():
         for c in range(3):
             start[:, c * lanes : (c + 1) * lanes] = q_ref[c]
-
-    local(v2[...], w3, fine_tab, f_acc)
-    for m, value3 in ((0, c0), (1, c1)):
-        local(saved[m], value3, coarse_tab, c_acc)
-        saved[3 + m] = finish(saved[m], coarse_tab, coarse_part, m, c_acc)
-    saved[2] = restrict(v2[...])
-    known = [restrict(rates[0]), restrict(rates[1])]
-    known.append(restrict(finish(v2[...], fine_tab, fine_part, 2, f_acc)))
+        start_halo[...] = f_recv[0]
+
+    local(v2[...], value3, fine_tab, f_acc.at[0])
+    for m in range(2):
+        saved[3 + m] = coarse_finish(saved[m], m, c_acc.at[m])
+    saved[2] = restrict(value3)
+    known = [restrict(stacked(rates[0])), restrict(stacked(rates[1]))]
+    known.append(restrict(stacked(finish(v2[...], fine_tab, arrive(fine_part, 2), f_acc.at[0]))))
     for m in range(2):
         row = QUAD_WEIGHTS[m]
         mixed = h * (row[0] * known[0] + row[1] * known[1] + row[2] * known[2])
@@ -302,11 +366,15 @@
         def _():
             term_copy(p, k).start()
 
+    @pl.when(p + 1 < slices)
+    def _():
+        handed()[1].start()
+
     @pl.when(p > 0)
     def _():
-        hand_on().wait_recv()
-
-    saved[5] = restrict(start[...])
+        handed()[0].wait_recv()
+
+    saved[5] = restrict(stacked(start[...]))
 
     @pl.when(p > 0)
     def _():
@@ -314,21 +382,52 @@
 
     seq[1] = terms[0]
 
+    def advance(value, r):
+        rate = coarse_finish(value, r + 2, c_acc.at[0])
+        seq[r + 2] = value + (0.5 * h) * rate + terms[r + 1]
+
+    def open_stage(r):
+        value = seq[r + 1]
+        value3 = stacked(value)
+        coarse_begin(value3, coarse_tab[1], r + 2)
+        local(value, value3, coarse_tab, c_acc.at[0])
+        return value
+
     def stage(r, carry):
-        value = seq[r + 1]
-        value3 = begin(value, coarse_tab, coarse_part, r + 2)
-        local(value, value3, coarse_tab, c_acc)
+        value = open_stage(r)
         source = (r + 1) // 2
 
         @pl.when((r % 2 == 1) & (source < p))
         def _():
             term_copy(source, 1).wait_recv()
 
-        rate = finish(value, coarse_tab, coarse_part, r + 2, c_acc)
-        seq[r + 2] = value + (0.5 * h) * rate + terms[r + 1]
+        advance(value, r)
         return carry
 
-    lax.fori_loop(0, 2 * p + 1, stage, 0)
+    lax.fori_loop(0, 2 * p, stage, 0)
+    value = open_stage(2 * p)
+
+    @pl.when(p > 0)
+    def _():
+        handed()[1].wait_recv()
+
+    wholes = ((start, saved.at[5]), (v1, saved.at[1]), (v2, saved.at[2]))
+
+    def correct(m):
+        whole, part = wholes[m]
+        delta = seq[2 * p + m] - part[...]
+        coarse_begin(stacked(delta), delta_faces, 2 * slices + 1 + m)
+        nodes[m] = whole[...] + prolong(delta)
+
+    for m in range(2):
+        correct(m)
+    advance(value, 2 * p)
+    correct(2)
+    for m in range(3):
+        local(nodes[m], stacked(nodes[m]), fine_tab, f_acc.at[m])
+    for m, base_halo in enumerate((start_halo, f_recv.at[1], f_recv.at[2])):
+        got = arrive(coarse_part, 2 * slices + 1 + m)
+        rates[m] = finish(nodes[m], fine_tab, base_halo[...] + prolong_halo(got), f_acc.at[m])
 
     for k in range(1, slices):
         @pl.when(p + k < slices)
@@ -337,23 +436,17 @@
 
     @pl.when(p + 1 < slices)
     def _():
-        hand_on().wait_send()
-
-    values3 = []
-    for m, (whole, part) in enumerate(((start, saved.at[5]), (v1, saved.at[1]), (v2, saved.at[2]))):
-        nodes[m] = whole[...] + prolong(seq[2 * p + m] - part[...])
-        values3.append(begin(nodes[m], fine_tab, fine_part, 3 + m))
-    for m in range(3):
-        local(nodes[m], values3[m], fine_tab, f_acc)
-        rates[m] = finish(nodes[m], fine_tab, fine_part, 3 + m, f_acc)
+        for copy in handed():
+            copy.wait_send()
 
     row = QUAD_WEIGHTS[0]
     v1[...] = nodes[0] + h * (row[0] * rates[0] + row[1] * rates[1] + row[2] * rates[2])
-    w3 = begin(v1[...], fine_tab, fine_part, 6)
-    local(v1[...], w3, fine_tab, f_acc)
+    value3 = stacked(v1[...])
+    begin(value3, 3)
+    local(v1[...], value3, fine_tab, f_acc.at[0])
     row = QUAD_WEIGHTS[1]
     v2[...] = v1[...] + h * (row[0] * rates[0] + (row[1] - 0.5) * rates[1] + row[2] * rates[2])
-    last = v2[...] + (0.5 * h) * finish(v1[...], fine_tab, fine_part, 6, f_acc)
+    last = v2[...] + (0.5 * h) * finish(v1[...], fine_tab, arrive(fine_part, 3), f_acc.at[0])
     for c in range(3):
         out_ref[c] = last[:, c * lanes : (c + 1) * lanes]
 
@@ -372,37 +465,55 @@
         up = interp_matrix(coarse_points, coarse_weights, fine_points)
         spread = lambda m, length: np.kron(np.eye(length // m.shape[1]), m)
         down_side, up_side = spread(down, side), spread(up, half)
+        fine_brick = lifted_matrix(FINE, side, False)
+        slope_of = [fine_brick[:1] @ up_side, fine_brick[-1:] @ up_side]
+        ident = np.eye(half)
+        delta_slopes = [np.kron(m, ident) for m in slope_of] + [np.kron(ident, m) for m in slope_of]
+        delta_values = face_rows(np.eye(half), half, True)[:4]
+        spots = np.eye(8)
+        halo_table = np.concatenate(
+            [np.kron(spots[j : j + 1], up_side) for d in range(4) for j in (d, 4 + d)]
+        )
+        up_z = spread(up, z_length // 2).T
+        down_z = spread(down, z_length).T
         tables = (
-            level_tables(FINE, side, z_length, lanes)
-            + level_tables(COARSE, half, z_length // 2, lanes)
+            level_tables(FINE, side, z_length, lanes, False)
+            + level_tables(COARSE, half, z_length // 2, lanes, True)
             + [
                 left_table(np.kron(down_side, down_side)),
-                right_table(padded(spread(down, z_length).T, lanes, lanes)),
+                right_table(np.tile(down_z, (1, 2))),
                 left_table(np.kron(up_side, up_side)),
-                right_table(padded(spread(up, z_length // 2).T, lanes, lanes)),
+                right_table(padded(up_z, lanes, lanes)),
+                left_table(np.concatenate(delta_values + delta_slopes)),
+                right_table(np.kron(np.eye(2), up_z)),
+                left_table(halo_table),
             ]
         )
         wide = 3 * lanes
-        fine_slots, coarse_slots = 7, 2 * slices + 1
+        fine_slots, coarse_slots = 4, 2 * slices + 4
         fine_field = pltpu.VMEM((fine_rows, wide), F32)
         geometry = (slices, bricks, fine_rows, coarse_rows, lanes)
         result = pl.pallas_call(
-            functools.partial(kernel, geometry),
+            functools.partial(kernel, geometry, len(tables)),
             out_shape=jax.ShapeDtypeStruct((3, fine_rows, lanes), F32),
-            in_specs=[pl.BlockSpec(memory_space=pltpu.VMEM)] * (1 + len(tables)),
+            in_specs=[pl.BlockSpec(memory_space=pltpu.HBM)] * (1 + len(tables)),
             out_specs=pl.BlockSpec(memory_space=pltpu.VMEM),
-            scratch_shapes=[
+            scratch_shapes=[pltpu.VMEM((3, fine_rows, lanes), F32)]
+            + [pltpu.VMEM(t.shape, BF16) for t in tables]
+            + [
+                pltpu.SemaphoreType.DMA((len(tables) + 1,)),
                 fine_field,
                 fine_field,
                 fine_field,
+                pltpu.VMEM((8 * side, wide), F32),
                 pltpu.VMEM((3, fine_rows, wide), F32),
                 pltpu.VMEM((3, fine_rows, wide), F32),
                 pltpu.VMEM((fine_slots, 8 * side, wide), F32),
                 pltpu.VMEM((fine_slots, 8 * side, wide), F32),
-                pltpu.VMEM((3 * fine_rows, 2 * wide), F32),
-                pltpu.VMEM((coarse_slots, 8 * half, wide), F32),
-                pltpu.VMEM((coarse_slots, 8 * half, wide), F32),
-                pltpu.VMEM((3 * coarse_rows, 2 * wide), F32),
+                pltpu.VMEM((3, 3 * fine_rows, 2 * wide), F32),
+                pltpu.VMEM((coarse_slots, 4 * half, wide), F32),
+                pltpu.VMEM((coarse_slots, 4 * half, wide), F32),
+                pltpu.VMEM((2, 3 * coarse_rows, 2 * wide), F32),
                 pltpu.VMEM((2 * slices + 1, coarse_rows, wide), F32),
                 pltpu.VMEM((2 * slices, coarse_rows, wide), F32),
                 pltpu.VMEM((6, coarse_rows, wide), F32),
@@ -412,11 +523,11 @@
                 pltpu.SemaphoreType.DMA((coarse_slots, 4)),
                 pltpu.SemaphoreType.DMA((slices,)),
                 pltpu.SemaphoreType.DMA((slices,)),
-                pltpu.SemaphoreType.DMA,
-                pltpu.SemaphoreType.DMA,
+                pltpu.SemaphoreType.DMA((2,)),
+                pltpu.SemaphoreType.DMA((2,)),
             ],
             compiler_params=pltpu.CompilerParams(
-                collective_id=0, has_side_effects=True, vmem_limit_bytes=40 * 2**20
+                collective_id=0, has_side_effects=True, vmem_limit_bytes=48 * 2**20
             ),
         )(initial.reshape(3, fine_rows, lanes), *[jnp.asarray(t) for t in tables])
         return result.reshape(initial.shape)

time: 93.5 us -> 86.5 us (0.925)
  the two profiles are of different devices: /device:TPU:5 before, /device:TPU:4 now
where the time goes in v1:
time: 86.5 us; the launch traced here: 85.8 us
  Pallas kernels  70.3 us (81%)
  local copies, waits for them, and re-layouts  15.5 us (18%)
    pallas_call x1, Pallas kernels, shards(): pl.pallas_call(functools.partial(kernel, geometry, len(tables)), out_shap...  70.3 us
    unnamed x33, local copies, waits for them, and re-layouts  15.5 us

profile of v1, /device:TPU:4, one launch (start us, length us, event | category | flops | bytes accessed | tf_op | source)
XLA Modules:
  0.0 85.8 jit_solution(9508970809724795438)
XLA Ops:
  0.0 0.0 copy-start
  0.0 1.3 %copy-done = bf16[768,768]{1,0:T(8,128)(2,1)S(1)} copy-done((bf16[768,768]{1,0:T(8,128)(2,1)S(1)}, bf16[768,768]{1,0:T(8,128)(2,1)}, u32[]{:S(2)}) %copy-start) | copy-done | bytes 1179672
  1.3 0.0 copy-start.1
  1.3 1.1 %copy-done.1 = bf16[768,384]{1,0:T(8,128)(2,1)S(1)} copy-done((bf16[768,384]{1,0:T(8,128)(2,1)S(1)}, bf16[768,384]{1,0:T(8,128)(2,1)}, u32[]{:S(2)}) %copy-start.1) | copy-done | bytes 589848
  2.3 0.0 copy-start.2
  2.3 1.0 %copy-done.2 = f32[1,3,1,16,16,128]{5,4,3,2,1,0:T(8,128)S(1)} copy-done((f32[1,3,1,16,16,128]{5,4,3,2,1,0:T(8,128)S(1)}, f32[1,3,1,16,16,128]{5,4,3,2,1,0:T(8,128)}, u32[]{:S(2)}) %copy-start.2) | copy-done | bytes 393240
  3.3 0.0 copy-start.3
  3.3 0.9 %copy-done.3 = bf16[384,256]{1,0:T(8,128)(2,1)S(1)} copy-done((bf16[384,256]{1,0:T(8,128)(2,1)S(1)}, bf16[384,256]{1,0:T(8,128)(2,1)}, u32[]{:S(2)}) %copy-start.3) | copy-done | bytes 196632
  4.3 0.0 copy-start.4
  4.3 0.9 %copy-done.4 = bf16[384,256]{1,0:T(8,128)(2,1)S(1)} copy-done((bf16[384,256]{1,0:T(8,128)(2,1)S(1)}, bf16[384,256]{1,0:T(8,128)(2,1)}, u32[]{:S(2)}) %copy-start.4) | copy-done | bytes 196632
  5.2 0.0 copy-start.5
  5.2 0.9 %copy-done.5 = bf16[384,256]{1,0:T(8,128)(2,1)S(1)} copy-done((bf16[384,256]{1,0:T(8,128)(2,1)S(1)}, bf16[384,256]{1,0:T(8,128)(2,1)}, u32[]{:S(2)}) %copy-start.5) | copy-done | bytes 196632
  6.1 0.0 copy-start.6
  6.1 0.9 %copy-done.6 = bf16[128,768]{1,0:T(8,128)(2,1)S(1)} copy-done((bf16[128,768]{1,0:T(8,128)(2,1)S(1)}, bf16[128,768]{1,0:T(8,128)(2,1)}, u32[]{:S(2)}) %copy-start.6) | copy-done | bytes 196632
  7.0 0.0 copy-start.7
  7.0 0.9 %copy-done.7 = bf16[256,192]{1,0:T(8,128)(2,1)S(1)} copy-done((bf16[256,192]{1,0:T(8,128)(2,1)S(1)}, bf16[256,192]{1,0:T(8,128)(2,1)}, u32[]{:S(2)}) %copy-start.7) | copy-done | bytes 98328
  7.9 0.0 copy-start.8
  7.9 0.9 %copy-done.8 = bf16[384,128]{1,0:T(8,128)(2,1)S(1)} copy-done((bf16[384,128]{1,0:T(8,128)(2,1)S(1)}, bf16[384,128]{1,0:T(8,128)(2,1)}, u32[]{:S(2)}) %copy-start.8) | copy-done | bytes 98328
  8.8 0.0 copy-start.9
  8.8 0.9 %copy-done.9 = bf16[384,128]{1,0:T(8,128)(2,1)S(1)} copy-done((bf16[384,128]{1,0:T(8,128)(2,1)S(1)}, bf16[384,128]{1,0:T(8,128)(2,1)}, u32[]{:S(2)}) %copy-start.9) | copy-done | bytes 98328
  9.7 0.0 copy-start.10
  9.7 0.9 %copy-done.10 = bf16[64,768]{1,0:T(8,128)(2,1)S(1)} copy-done((bf16[64,768]{1,0:T(8,128)(2,1)S(1)}, bf16[64,768]{1,0:T(8,128)(2,1)}, u32[]{:S(2)}) %copy-start.10) | copy-done | bytes 98328
  10.6 0.0 copy-start.11
  10.6 0.9 %copy-done.11 = bf16[192,192]{1,0:T(8,128)(2,1)S(1)} copy-done((bf16[192,192]{1,0:T(8,128)(2,1)S(1)}, bf16[192,192]{1,0:T(8,128)(2,1)}, u32[]{:S(2)}) %copy-start.11) | copy-done | bytes 73752
  11.5 0.0 copy-start.12
  11.5 0.9 %copy-done.12 = bf16[192,192]{1,0:T(8,128)(2,1)S(1)} copy-done((bf16[192,192]{1,0:T(8,128)(2,1)S(1)}, bf16[192,192]{1,0:T(8,128)(2,1)}, u32[]{:S(2)}) %copy-start.12) | copy-done | bytes 73752
  12.4 0.0 copy-start.13
  12.4 0.8 copy-done.13
  13.3 0.8 copy-done.14
  14.0 0.8 copy-done.15
  14.8 70.3 %shard_map.154 = f32[3,256,128]{2,1,0:T(8,128)S(1)} custom-call(f32[3,256,128]{2,1,0:T(8,128)S(1)} %bitcast.5, bf16[768,768]{1,0:T(8,128)(2,1)S(1)} %copy-done, bf16[128,768]{1,0:T(8,128)(2,1)S(1)} %copy-done.6, bf16[768,384]{1,0:T(8,128)(2,1)S(1)} %copy-done.1, bf16[384,256]{1,0:T(8,128)(2,1)S(1)} %copy-done.5, bf16[192,192]{1,0:T(8,128)(2,1)S(1)} %copy-done.12, ...), custom_call_target="tpu_custom_call" | custom-call | tf_op jit(solution)/shard_map/pallas_call | solution.py:496
  85.0 0.7 copy.19
  (2 shorter events, 0.0 us)
Async XLA Ops:
  0.0 1.3 %copy-start = (bf16[768,768]{1,0:T(8,128)(2,1)S(1)}, bf16[768,768]{1,0:T(8,128)(2,1)}, u32[]{:S(2)}) copy-start(bf16[768,768]{1,0:T(8,128)(2,1)} %constant.30.clone.refs_0_) | copy-start | bytes 3538948
  1.3 1.1 %copy-start.1 = (bf16[768,384]{1,0:T(8,128)(2,1)S(1)}, bf16[768,384]{1,0:T(8,128)(2,1)}, u32[]{:S(2)}) copy-start(bf16[768,384]{1,0:T(8,128)(2,1)} %constant.32.clone.refs_2_) | copy-start | bytes 1769476
  2.3 1.0 %copy-start.2 = (f32[1,3,1,16,16,128]{5,4,3,2,1,0:T(8,128)S(1)}, f32[1,3,1,16,16,128]{5,4,3,2,1,0:T(8,128)}, u32[]{:S(2)}) copy-start(f32[1,3,1,16,16,128]{5,4,3,2,1,0:T(8,128)} %param.16) | copy-start | bytes 1179652
  3.3 0.9 %copy-start.3 = (bf16[384,256]{1,0:T(8,128)(2,1)S(1)}, bf16[384,256]{1,0:T(8,128)(2,1)}, u32[]{:S(2)}) copy-start(bf16[384,256]{1,0:T(8,128)(2,1)} %constant.43.clone.refs_13_) | copy-start | bytes 589828
  4.3 0.9 %copy-start.4 = (bf16[384,256]{1,0:T(8,128)(2,1)S(1)}, bf16[384,256]{1,0:T(8,128)(2,1)}, u32[]{:S(2)}) copy-start(bf16[384,256]{1,0:T(8,128)(2,1)} %constant.37.clone.refs_7_) | copy-start | bytes 589828
  5.2 0.9 %copy-start.5 = (bf16[384,256]{1,0:T(8,128)(2,1)S(1)}, bf16[384,256]{1,0:T(8,128)(2,1)}, u32[]{:S(2)}) copy-start(bf16[384,256]{1,0:T(8,128)(2,1)} %constant.33.clone.refs_3_) | copy-start | bytes 589828
  6.1 0.9 %copy-start.6 = (bf16[128,768]{1,0:T(8,128)(2,1)S(1)}, bf16[128,768]{1,0:T(8,128)(2,1)}, u32[]{:S(2)}) copy-start(bf16[128,768]{1,0:T(8,128)(2,1)} %constant.31.clone.refs_1_) | copy-start | bytes 589828
  7.0 0.9 %copy-start.7 = (bf16[256,192]{1,0:T(8,128)(2,1)S(1)}, bf16[256,192]{1,0:T(8,128)(2,1)}, u32[]{:S(2)}) copy-start(bf16[256,192]{1,0:T(8,128)(2,1)} %constant.40.clone.refs_10_) | copy-start | bytes 294916
  7.9 0.9 %copy-start.8 = (bf16[384,128]{1,0:T(8,128)(2,1)S(1)}, bf16[384,128]{1,0:T(8,128)(2,1)}, u32[]{:S(2)}) copy-start(bf16[384,128]{1,0:T(8,128)(2,1)} %constant.41.clone.refs_11_) | copy-start | bytes 294916
  8.8 0.9 %copy-start.9 = (bf16[384,128]{1,0:T(8,128)(2,1)S(1)}, bf16[384,128]{1,0:T(8,128)(2,1)}, u32[]{:S(2)}) copy-start(bf16[384,128]{1,0:T(8,128)(2,1)} %constant.39.clone.refs_9_) | copy-start | bytes 294916
  9.7 0.9 %copy-start.10 = (bf16[64,768]{1,0:T(8,128)(2,1)S(1)}, bf16[64,768]{1,0:T(8,128)(2,1)}, u32[]{:S(2)}) copy-start(bf16[64,768]{1,0:T(8,128)(2,1)} %constant.38.clone.refs_8_) | copy-start | bytes 294916
  10.6 0.9 %copy-start.11 = (bf16[192,192]{1,0:T(8,128)(2,1)S(1)}, bf16[192,192]{1,0:T(8,128)(2,1)}, u32[]{:S(2)}) copy-start(bf16[192,192]{1,0:T(8,128)(2,1)} %constant.36.clone.refs_6_) | copy-start | bytes 221188
  11.5 0.9 %copy-start.12 = (bf16[192,192]{1,0:T(8,128)(2,1)S(1)}, bf16[192,192]{1,0:T(8,128)(2,1)}, u32[]{:S(2)}) copy-start(bf16[192,192]{1,0:T(8,128)(2,1)} %constant.34.clone.refs_4_) | copy-start | bytes 221188
  12.4 0.8 copy-start.13
  13.3 0.8 copy-start.14
  14.0 0.8 copy-start.15

commit v2 on v1

--- a/solution.py
+++ b/solution.py
@@ -17,6 +17,7 @@
 MESH = pl.DeviceIdType.MESH
 F32 = jnp.float32
 BF16 = jnp.bfloat16
+VMEM_LIMIT = 62 * 2**20
 
 
 def cheb_tables(count):
@@ -145,7 +146,7 @@
 
 
 def left(table, value3):
-    return jnp.dot(table[...], value3, preferred_element_type=F32)
+    return jnp.dot(table[:, : value3.shape[0]], value3, preferred_element_type=F32)
 
 
 def right(value, table, lanes):
@@ -161,9 +162,10 @@
     return jnp.concatenate([value[at : at + rows] for at in range(0, value.shape[0], rows)], axis=1)
 
 
-def kernel(geometry, table_count, q_hbm, *refs):
+def kernel(geometry, places, q_hbm, *refs):
     slices, bricks, fine_rows, coarse_rows, lanes = geometry
-    sources, refs = refs[:table_count], refs[table_count:]
+    table_count = len(places)
+    sources, refs = refs[:2], refs[2:]
     out_ref, q_ref, refs = refs[0], refs[1], refs[2:]
     tables, refs = refs[:table_count], refs[table_count:]
     fine_tab, coarse_tab = tables[:4], tables[4:8]
@@ -178,7 +180,11 @@
     q_load.start()
     loads = {}
     for i in (1, 0, 3, 2, 8, 9, 5, 4, 7, 6, 10, 11, 12, 13, 14):
-        loads[i] = pltpu.make_async_copy(sources[i], tables[i], l_sem.at[i])
+        bank, at = places[i]
+        rows, columns = tables[i].shape
+        loads[i] = pltpu.make_async_copy(
+            sources[bank].at[pl.ds(at, rows), pl.ds(0, columns)], tables[i], l_sem.at[i]
+        )
         loads[i].start()
 
     p = lax.axis_index("tm")
@@ -325,11 +331,12 @@
             device_id_type=MESH,
         )
 
-    handed = lambda: (hand_on(v2, start, 0), hand_on(f_recv.at[2], start_halo, 1))
+    hand_state = lambda: hand_on(v2, start, 0)
+    hand_halo = lambda: hand_on(f_recv.at[2], start_halo, 1)
 
     @pl.when(p + 1 < slices)
     def _():
-        handed()[0].start()
+        hand_state().start()
 
     @pl.when(p == 0)
     def _():
@@ -343,18 +350,18 @@
     saved[2] = restrict(value3)
     known = [restrict(stacked(rates[0])), restrict(stacked(rates[1]))]
     known.append(restrict(stacked(finish(v2[...], fine_tab, arrive(fine_part, 2), f_acc.at[0]))))
-    for m in range(2):
-        row = QUAD_WEIGHTS[m]
-        mixed = h * (row[0] * known[0] + row[1] * known[1] + row[2] * known[2])
-        if m == 0:
-            terms[2 * p] = mixed + jnp.where(p == 0, saved[0], (-0.5 * h) * saved[3])
-        else:
-            terms[2 * p + 1] = mixed - (0.5 * h) * saved[4]
+    first, second = [
+        h * (row[0] * known[0] + row[1] * known[1] + row[2] * known[2]) for row in QUAD_WEIGHTS
+    ]
+    first = first + jnp.where(p == 0, saved[0], (-0.5 * h) * saved[3])
+    second = second - (0.5 * h) * saved[4]
+    low_field = lax.broadcasted_iota(jnp.int32, first.shape, 1) % lanes < half
+    terms[p] = jnp.where(low_field, first, second)
 
     def term_copy(source, k):
         return pltpu.make_async_remote_copy(
-            src_ref=terms.at[pl.ds(2 * source, 2)],
-            dst_ref=terms.at[pl.ds(2 * source, 2)],
+            src_ref=terms.at[source],
+            dst_ref=terms.at[source],
             send_sem=t_ssem.at[k],
             recv_sem=t_rsem.at[source],
             device_id={"tm": lax.rem(p + k, slices)},
@@ -366,25 +373,23 @@
         def _():
             term_copy(p, k).start()
 
-    @pl.when(p + 1 < slices)
-    def _():
-        handed()[1].start()
-
-    @pl.when(p > 0)
-    def _():
-        handed()[0].wait_recv()
-
-    saved[5] = restrict(stacked(start[...]))
-
     @pl.when(p > 0)
     def _():
         term_copy(0, 1).wait_recv()
 
-    seq[1] = terms[0]
+    def term(source, which):
+        both = terms[source]
+        turned = jnp.concatenate(
+            [pltpu.roll(both[:, c * lanes : (c + 1) * lanes], half, 1) for c in range(3)], axis=1
+        )
+        straight = jnp.where(low_field, 0, 1) == which
+        return jnp.where(straight, both, turned)
+
+    seq[1] = term(0, 0)
 
     def advance(value, r):
-        rate = coarse_finish(value, r + 2, c_acc.at[0])
-        seq[r + 2] = value + (0.5 * h) * rate + terms[r + 1]
+        known = value + term((r + 1) // 2, (r + 1) % 2)
+        seq[r + 2] = known + (0.5 * h) * coarse_finish(value, r + 2, c_acc.at[0])
 
     def open_stage(r):
         value = seq[r + 1]
@@ -407,9 +412,16 @@
     lax.fori_loop(0, 2 * p, stage, 0)
     value = open_stage(2 * p)
 
+    @pl.when(p + 1 < slices)
+    def _():
+        hand_halo().start()
+
     @pl.when(p > 0)
     def _():
-        handed()[1].wait_recv()
+        hand_state().wait_recv()
+        hand_halo().wait_recv()
+
+    saved[5] = restrict(stacked(start[...]))
 
     wholes = ((start, saved.at[5]), (v1, saved.at[1]), (v2, saved.at[2]))
 
@@ -436,8 +448,8 @@
 
     @pl.when(p + 1 < slices)
     def _():
-        for copy in handed():
-            copy.wait_send()
+        hand_state().wait_send()
+        hand_halo().wait_send()
 
     row = QUAD_WEIGHTS[0]
     v1[...] = nodes[0] + h * (row[0] * rates[0] + row[1] * rates[1] + row[2] * rates[2])
@@ -490,13 +502,21 @@
             ]
         )
         wide = 3 * lanes
+        tables = [padded(t, t.shape[0], -(-t.shape[1] // lanes) * lanes) for t in tables]
+        banks, places = ([], []), []
+        for t in tables:
+            bank = int(t.shape[1] <= wide)
+            places.append((bank, sum(len(other) for other in banks[bank])))
+            width = wide if bank else tables[0].shape[1]
+            banks[bank].append(padded(t, t.shape[0], width))
+        banks = [np.concatenate(bank) for bank in banks]
         fine_slots, coarse_slots = 4, 2 * slices + 4
         fine_field = pltpu.VMEM((fine_rows, wide), F32)
         geometry = (slices, bricks, fine_rows, coarse_rows, lanes)
         result = pl.pallas_call(
-            functools.partial(kernel, geometry, len(tables)),
+            functools.partial(kernel, geometry, places),
             out_shape=jax.ShapeDtypeStruct((3, fine_rows, lanes), F32),
-            in_specs=[pl.BlockSpec(memory_space=pltpu.HBM)] * (1 + len(tables)),
+            in_specs=[pl.BlockSpec(memory_space=pl.ANY)] * 3,
             out_specs=pl.BlockSpec(memory_space=pltpu.VMEM),
             scratch_shapes=[pltpu.VMEM((3, fine_rows, lanes), F32)]
             + [pltpu.VMEM(t.shape, BF16) for t in tables]
@@ -515,7 +535,7 @@
                 pltpu.VMEM((coarse_slots, 4 * half, wide), F32),
                 pltpu.VMEM((2, 3 * coarse_rows, 2 * wide), F32),
                 pltpu.VMEM((2 * slices + 1, coarse_rows, wide), F32),
-                pltpu.VMEM((2 * slices, coarse_rows, wide), F32),
+                pltpu.VMEM((slices, coarse_rows, wide), F32),
                 pltpu.VMEM((6, coarse_rows, wide), F32),
                 pltpu.SemaphoreType.DMA((fine_slots, 4)),
                 pltpu.SemaphoreType.DMA((fine_slots, 4)),
@@ -527,9 +547,9 @@
                 pltpu.SemaphoreType.DMA((2,)),
             ],
             compiler_params=pltpu.CompilerParams(
-                collective_id=0, has_side_effects=True, vmem_limit_bytes=48 * 2**20
+                collective_id=0, has_side_effects=True, vmem_limit_bytes=VMEM_LIMIT
             ),
-        )(initial.reshape(3, fine_rows, lanes), *[jnp.asarray(t) for t in tables])
+        )(initial.reshape(3, fine_rows, lanes), *[jnp.asarray(bank) for bank in banks])
         return result.reshape(initial.shape)
 
     return jax.shard_map(

time: 86.5 us -> 67.5 us (0.78)
  the two profiles are of different devices: /device:TPU:4 before, /device:TPU:5 now
where the time goes in v2:
time: 67.5 us; the launch traced here: 67.4 us
  Pallas kernels  65.6 us (97%)
  local copies, waits for them, and re-layouts  1.77 us (3%)
    pallas_call x1, Pallas kernels, shards(): pl.pallas_call(functools.partial(kernel, geometry, places), out_shape=jax...  65.6 us
    unnamed x1, local copies, waits for them, and re-layouts  1.77 us

profile of v2, /device:TPU:5, one launch (start us, length us, event | category | flops | bytes accessed | tf_op | source)
XLA Modules:
  0.0 67.4 jit_solution(16592728504913796562)
XLA Ops:
  0.0 65.6 %shard_map.37 = f32[3,256,128]{2,1,0:T(8,128)} custom-call(f32[3,256,128]{2,1,0:T(8,128)} %bitcast.5, bf16[960,768]{1,0:T(8,128)(2,1)} %constant.4.clone.refs_0_, bf16[3584,384]{1,0:T(8,128)(2,1)} %constant.5.clone.refs_1_), custom_call_target="tpu_custom_call" | custom-call | tf_op jit(solution)/shard_map/pallas_call | solution.py:516
  65.6 1.8 %copy.6 = f32[1,3,1,16,16,128]{5,4,3,2,1,0:T(8,128)} copy(f32[1,3,1,16,16,128]{5,4,3,2,1,0:T(8,128)} %bitcast.4) | data formatting | bytes 786432

commit v3 on v2

--- a/solution.py
+++ b/solution.py
@@ -17,7 +17,8 @@
 MESH = pl.DeviceIdType.MESH
 F32 = jnp.float32
 BF16 = jnp.bfloat16
-VMEM_LIMIT = 62 * 2**20
+VMEM_LIMIT = 52 * 2**20
+BANK_SPARE = 5504
 
 
 def cheb_tables(count):
@@ -165,7 +166,7 @@
 def kernel(geometry, places, q_hbm, *refs):
     slices, bricks, fine_rows, coarse_rows, lanes = geometry
     table_count = len(places)
-    sources, refs = refs[:2], refs[2:]
+    bank, refs = refs[0], refs[1:]
     out_ref, q_ref, refs = refs[0], refs[1], refs[2:]
     tables, refs = refs[:table_count], refs[table_count:]
     fine_tab, coarse_tab = tables[:4], tables[4:8]
@@ -180,10 +181,10 @@
     q_load.start()
     loads = {}
     for i in (1, 0, 3, 2, 8, 9, 5, 4, 7, 6, 10, 11, 12, 13, 14):
-        bank, at = places[i]
+        row, column = places[i]
         rows, columns = tables[i].shape
         loads[i] = pltpu.make_async_copy(
-            sources[bank].at[pl.ds(at, rows), pl.ds(0, columns)], tables[i], l_sem.at[i]
+            bank.at[pl.ds(row, rows), pl.ds(column, columns)], tables[i], l_sem.at[i]
         )
         loads[i].start()
 
@@ -207,28 +208,45 @@
         )
     pl.semaphore_wait(barrier, 4 + slices - 1)
 
+    def face_copy(send, recv, ssem, rsem, slot, d, at, rows, which):
+        size = send.shape[1] // 4
+        return pltpu.make_async_remote_copy(
+            src_ref=send.at[slot, pl.ds(d * size + at, rows)],
+            dst_ref=recv.at[slot, pl.ds(landing[d] * size + at, rows)],
+            send_sem=ssem.at[slot, 4 * which + d],
+            recv_sem=rsem.at[slot, 4 * which + landing[d]],
+            device_id={"space": targets[d]},
+            device_id_type=MESH,
+        )
+
     def copies(send, recv, ssem, rsem, slot):
         size = send.shape[1] // 4
-        return [
-            pltpu.make_async_remote_copy(
-                src_ref=send.at[slot, pl.ds(d * size, size)],
-                dst_ref=recv.at[slot, pl.ds(landing[d] * size, size)],
-                send_sem=ssem.at[slot, d],
-                recv_sem=rsem.at[slot, landing[d]],
-                device_id={"space": targets[d]},
-                device_id_type=MESH,
-            )
-            for d in range(4)
-        ]
+        parts = (send, recv, ssem, rsem, slot)
+        if send is not f_send:
+            return [face_copy(*parts, d, 0, size, 0) for d in range(4)]
+        return [face_copy(*parts, d, 0, size // 2, 0) for d in range(2)] + [
+            face_copy(*parts, d, size // 2, size // 2, 1) for d in range(2)
+        ] + [face_copy(*parts, d, 0, size, 0) for d in range(2, 4)]
 
     fine_part = (f_send, f_recv, f_ssem, f_rsem)
     coarse_part = (c_send, c_recv, c_ssem, c_rsem)
     low_lanes = lax.broadcasted_iota(jnp.int32, (size, 3 * lanes), 1) % lanes < half
 
-    def begin(value3, slot):
-        f_send[slot] = left(fine_tab[1], value3)
-        for copy in copies(*fine_part, slot):
+    face = f_send.shape[1] // 8
+
+    def begin(value, slot):
+        parts = copies(*fine_part, slot)
+        f_send[slot, :face] = value[:face]
+        f_send[slot, 2 * face : 3 * face] = value[-face:]
+        for copy in parts[:2]:
             copy.start()
+        value3 = stacked(value)
+        faces = left(fine_tab[1], value3)
+        f_send[slot, face : 2 * face] = faces[face : 2 * face]
+        f_send[slot, 3 * face :] = faces[3 * face :]
+        for copy in parts[2:]:
+            copy.start()
+        return value3
 
     def coarse_begin(value3, table, slot):
         faces = left(table, value3)
@@ -293,9 +311,8 @@
     h = TIME_STEP
     q_load.wait()
     q = jnp.concatenate([q_ref[c] for c in range(3)], axis=1)
-    value3 = stacked(q)
     loads[1].wait()
-    begin(value3, 0)
+    value3 = begin(q, 0)
     for i in (0, 3):
         loads[i].wait()
     local(q, value3, fine_tab, f_acc.at[0])
@@ -306,8 +323,7 @@
     rates[0] = finish(q, fine_tab, arrive(fine_part, 0), f_acc.at[0])
 
     v1[...] = q + (0.5 * h) * rates[0]
-    value3 = stacked(v1[...])
-    begin(value3, 1)
+    value3 = begin(v1[...], 1)
     saved[1] = restrict(value3)
     for i in (4, 5, 6, 7, 10, 11, 12, 13, 14):
         loads[i].wait()
@@ -318,8 +334,7 @@
     local(v1[...], value3, fine_tab, f_acc.at[0])
     rates[1] = finish(v1[...], fine_tab, arrive(fine_part, 1), f_acc.at[0])
     v2[...] = v1[...] + (0.5 * h) * rates[1]
-    value3 = stacked(v2[...])
-    begin(value3, 2)
+    value3 = begin(v2[...], 2)
 
     def hand_on(source, target, which):
         return pltpu.make_async_remote_copy(
@@ -398,31 +413,6 @@
         local(value, value3, coarse_tab, c_acc.at[0])
         return value
 
-    def stage(r, carry):
-        value = open_stage(r)
-        source = (r + 1) // 2
-
-        @pl.when((r % 2 == 1) & (source < p))
-        def _():
-            term_copy(source, 1).wait_recv()
-
-        advance(value, r)
-        return carry
-
-    lax.fori_loop(0, 2 * p, stage, 0)
-    value = open_stage(2 * p)
-
-    @pl.when(p + 1 < slices)
-    def _():
-        hand_halo().start()
-
-    @pl.when(p > 0)
-    def _():
-        hand_state().wait_recv()
-        hand_halo().wait_recv()
-
-    saved[5] = restrict(stacked(start[...]))
-
     wholes = ((start, saved.at[5]), (v1, saved.at[1]), (v2, saved.at[2]))
 
     def correct(m):
@@ -430,13 +420,48 @@
         delta = seq[2 * p + m] - part[...]
         coarse_begin(stacked(delta), delta_faces, 2 * slices + 1 + m)
         nodes[m] = whole[...] + prolong(delta)
-
-    for m in range(2):
-        correct(m)
+        local(nodes[m], stacked(nodes[m]), fine_tab, f_acc.at[m])
+
+    def stage(r, carry):
+        value = open_stage(r)
+        source = (r + 1) // 2
+
+        @pl.when((r % 2 == 1) & (source < p))
+        def _():
+            term_copy(source, 1).wait_recv()
+
+        @pl.when(r == 2 * p - 2)
+        def _():
+            hand_state().wait_recv()
+            saved[5] = restrict(stacked(start[...]))
+
+        @pl.when(r == 2 * p - 1)
+        def _():
+            correct(0)
+
+        advance(value, r)
+        return carry
+
+    lax.fori_loop(0, 2 * p, stage, 0)
+    value = open_stage(2 * p)
+
+    @pl.when(p + 1 < slices)
+    def _():
+        hand_halo().start()
+
+    @pl.when(p == 0)
+    def _():
+        saved[5] = restrict(stacked(start[...]))
+        correct(0)
+
+    correct(1)
     advance(value, 2 * p)
     correct(2)
-    for m in range(3):
-        local(nodes[m], stacked(nodes[m]), fine_tab, f_acc.at[m])
+
+    @pl.when(p > 0)
+    def _():
+        hand_halo().wait_recv()
+
     for m, base_halo in enumerate((start_halo, f_recv.at[1], f_recv.at[2])):
         got = arrive(coarse_part, 2 * slices + 1 + m)
         rates[m] = finish(nodes[m], fine_tab, base_halo[...] + prolong_halo(got), f_acc.at[m])
@@ -453,8 +478,7 @@
 
     row = QUAD_WEIGHTS[0]
     v1[...] = nodes[0] + h * (row[0] * rates[0] + row[1] * rates[1] + row[2] * rates[2])
-    value3 = stacked(v1[...])
-    begin(value3, 3)
+    value3 = begin(v1[...], 3)
     local(v1[...], value3, fine_tab, f_acc.at[0])
     row = QUAD_WEIGHTS[1]
     v2[...] = v1[...] + h * (row[0] * rates[0] + (row[1] - 0.5) * rates[1] + row[2] * rates[2])
@@ -503,20 +527,24 @@
         )
         wide = 3 * lanes
         tables = [padded(t, t.shape[0], -(-t.shape[1] // lanes) * lanes) for t in tables]
-        banks, places = ([], []), []
-        for t in tables:
-            bank = int(t.shape[1] <= wide)
-            places.append((bank, sum(len(other) for other in banks[bank])))
-            width = wide if bank else tables[0].shape[1]
-            banks[bank].append(padded(t, t.shape[0], width))
-        banks = [np.concatenate(bank) for bank in banks]
+        bank_width = 2 * wide
+        places, heights = [], [0, 0]
+        for t in sorted(range(len(tables)), key=lambda t: -tables[t].shape[1]):
+            side_by = int(heights[1] < heights[0])
+            places.append((t, heights[side_by], side_by * wide))
+            for other in range(2) if tables[t].shape[1] > wide else (side_by,):
+                heights[other] += tables[t].shape[0]
+        places = [place[1:] for place in sorted(places)]
+        bank = np.zeros((max(heights) + BANK_SPARE, bank_width), jnp.bfloat16)
+        for t, (row, column) in zip(tables, places):
+            bank[row : row + t.shape[0], column : column + t.shape[1]] = t
         fine_slots, coarse_slots = 4, 2 * slices + 4
         fine_field = pltpu.VMEM((fine_rows, wide), F32)
         geometry = (slices, bricks, fine_rows, coarse_rows, lanes)
         result = pl.pallas_call(
             functools.partial(kernel, geometry, places),
             out_shape=jax.ShapeDtypeStruct((3, fine_rows, lanes), F32),
-            in_specs=[pl.BlockSpec(memory_space=pl.ANY)] * 3,
+            in_specs=[pl.BlockSpec(memory_space=pl.ANY)] * 2,
             out_specs=pl.BlockSpec(memory_space=pltpu.VMEM),
             scratch_shapes=[pltpu.VMEM((3, fine_rows, lanes), F32)]
             + [pltpu.VMEM(t.shape, BF16) for t in tables]
@@ -537,8 +565,8 @@
                 pltpu.VMEM((2 * slices + 1, coarse_rows, wide), F32),
                 pltpu.VMEM((slices, coarse_rows, wide), F32),
                 pltpu.VMEM((6, coarse_rows, wide), F32),
-                pltpu.SemaphoreType.DMA((fine_slots, 4)),
-                pltpu.SemaphoreType.DMA((fine_slots, 4)),
+                pltpu.SemaphoreType.DMA((fine_slots, 8)),
+                pltpu.SemaphoreType.DMA((fine_slots, 8)),
                 pltpu.SemaphoreType.DMA((coarse_slots, 4)),
                 pltpu.SemaphoreType.DMA((coarse_slots, 4)),
                 pltpu.SemaphoreType.DMA((slices,)),
@@ -549,7 +577,7 @@
             compiler_params=pltpu.CompilerParams(
                 collective_id=0, has_side_effects=True, vmem_limit_bytes=VMEM_LIMIT
             ),
-        )(initial.reshape(3, fine_rows, lanes), *[jnp.asarray(bank) for bank in banks])
+        )(initial.reshape(3, fine_rows, lanes), jnp.asarray(bank))
         return result.reshape(initial.shape)
 
     return jax.shard_map(

time: 67.5 us -> 65.1 us (0.964)
  Pallas kernels: 65.6 us -> 63.2 us
    pallas_call x1, Pallas kernels: 65.6 us -> 63.2 us  [shards(): pl.pallas_call(functools.partial(kernel, geometry, places), out_shape=jax...]
    unnamed x1 -> x3, local copies, waits for them, and re-layouts: 1.77 us -> 1.74 us
where the time goes in v3:
time: 65.1 us; the launch traced here: 65 us
  Pallas kernels  63.2 us (97%)
  local copies, waits for them, and re-layouts  1.74 us (3%)
    pallas_call x1, Pallas kernels, shards(): pl.pallas_call(functools.partial(kernel, geometry, places), out_shape=jax...  63.2 us
    unnamed x3, local copies, waits for them, and re-layouts  1.74 us

profile of v3, /device:TPU:5, one launch (start us, length us, event | category | flops | bytes accessed | tf_op | source)
XLA Modules:
  0.0 65.0 jit_solution(787931512742545962)
XLA Ops:
  0.0 0.0 copy-start
  0.0 1.0 %copy-done = f32[1,3,1,16,16,128]{5,4,3,2,1,0:T(8,128)S(1)} copy-done((f32[1,3,1,16,16,128]{5,4,3,2,1,0:T(8,128)S(1)}, f32[1,3,1,16,16,128]{5,4,3,2,1,0:T(8,128)}, u32[]{:S(2)}) %copy-start) | copy-done | bytes 393240
  1.0 63.2 %shard_map.28 = f32[3,256,128]{2,1,0:T(8,128)S(1)} custom-call(f32[3,256,128]{2,1,0:T(8,128)S(1)} %bitcast.5, bf16[8384,768]{1,0:T(8,128)(2,1)} %constant.2.clone.refs_0_), custom_call_target="tpu_custom_call" | custom-call | tf_op jit(solution)/shard_map/pallas_call | solution.py:544
  64.2 0.7 %copy.5 = f32[1,3,1,16,16,128]{5,4,3,2,1,0:T(8,128)} copy(f32[1,3,1,16,16,128]{5,4,3,2,1,0:T(8,128)S(1)} %bitcast.4) | data formatting | bytes 786432
Async XLA Ops:
  0.0 1.0 %copy-start = (f32[1,3,1,16,16,128]{5,4,3,2,1,0:T(8,128)S(1)}, f32[1,3,1,16,16,128]{5,4,3,2,1,0:T(8,128)}, u32[]{:S(2)}) copy-start(f32[1,3,1,16,16,128]{5,4,3,2,1,0:T(8,128)} %param.2) | copy-start | bytes 1179652

commit v4 on v3

--- a/solution.py
+++ b/solution.py
@@ -173,7 +173,8 @@
     (restrict_rows, restrict_z, prolong_rows, prolong_z,
      delta_faces, halo_z, halo_rows) = tables[8:]
     (l_sem, v1, v2, start, start_halo, rates, nodes, f_send, f_recv, f_acc, c_send, c_recv, c_acc,
-     seq, terms, saved, f_ssem, f_rsem, c_ssem, c_rsem, t_ssem, t_rsem, s_ssem, s_rsem) = refs
+     seq, terms, saved, f_ssem, f_rsem, c_ssem, c_rsem, t_ssem, t_rsem, s_ssem, s_rsem,
+     chain, k_ssem, k_rsem) = refs
     half = lanes // 2
     size = c_send.shape[1]
 
@@ -383,14 +384,32 @@
             device_id_type=MESH,
         )
 
-    for k in range(slices - 1, 0, -1):
-        @pl.when(p + k < slices)
-        def _():
-            term_copy(p, k).start()
-
-    @pl.when(p > 0)
-    def _():
-        term_copy(0, 1).wait_recv()
+    low_chain = low_field[: coarse_rows // 2]
+    odd = lax.rem(p, 2)
+    chip = p - odd
+    sends_term = (odd == 0) & (p + 1 < slices)
+
+    @pl.when(sends_term)
+    def _():
+        term_copy(p, 1).start()
+
+    @pl.when(odd == 1)
+    def _():
+        term_copy(p - 1, 1).wait_recv()
+
+    def chain_copy(k):
+        return pltpu.make_async_remote_copy(
+            src_ref=chain.at[0],
+            dst_ref=chain.at[1],
+            send_sem=k_ssem.at[k - 1],
+            recv_sem=k_rsem,
+            device_id={"tm": lax.rem(p + k, slices)},
+            device_id_type=MESH,
+        )
+
+    def take_start():
+        hand_state().wait_recv()
+        saved[5] = restrict(stacked(start[...]))
 
     def term(source, which):
         both = terms[source]
@@ -400,7 +419,20 @@
         straight = jnp.where(low_field, 0, 1) == which
         return jnp.where(straight, both, turned)
 
-    seq[1] = term(0, 0)
+    @pl.when(chip == 0)
+    def _():
+        seq[1] = term(0, 0)
+
+    @pl.when(chip > 0)
+    def _():
+        take_start()
+        chain_copy(1).wait_recv()
+        both = chain[1]
+        turned = jnp.concatenate(
+            [pltpu.roll(both[:, c * lanes : (c + 1) * lanes], half, 1) for c in range(3)], axis=1
+        )
+        seq[2 * chip, : coarse_rows // 2] = jnp.where(low_chain, both, turned)
+        seq[2 * chip, coarse_rows // 2 :] = jnp.where(low_chain, turned, both)
 
     def advance(value, r):
         known = value + term((r + 1) // 2, (r + 1) % 2)
@@ -424,16 +456,10 @@
 
     def stage(r, carry):
         value = open_stage(r)
-        source = (r + 1) // 2
-
-        @pl.when((r % 2 == 1) & (source < p))
+
+        @pl.when((chip == 0) & (r == 0))
         def _():
-            term_copy(source, 1).wait_recv()
-
-        @pl.when(r == 2 * p - 2)
-        def _():
-            hand_state().wait_recv()
-            saved[5] = restrict(stacked(start[...]))
+            take_start()
 
         @pl.when(r == 2 * p - 1)
         def _():
@@ -442,7 +468,7 @@
         advance(value, r)
         return carry
 
-    lax.fori_loop(0, 2 * p, stage, 0)
+    lax.fori_loop(jnp.maximum(2 * chip - 1, 0), 2 * p, stage, 0)
     value = open_stage(2 * p)
 
     @pl.when(p + 1 < slices)
@@ -456,6 +482,18 @@
 
     correct(1)
     advance(value, 2 * p)
+    chain_on = [(odd == 1) & (p + k < slices) for k in (1, 2)]
+
+    @pl.when(chain_on[0])
+    def _():
+        node = seq[2 * p + 2]
+        chain[0] = jnp.where(low_chain, node[: coarse_rows // 2], node[coarse_rows // 2 :])
+
+    for k in (2, 1):
+        @pl.when(chain_on[k - 1])
+        def _():
+            chain_copy(k).start()
+
     correct(2)
 
     @pl.when(p > 0)
@@ -466,10 +504,14 @@
         got = arrive(coarse_part, 2 * slices + 1 + m)
         rates[m] = finish(nodes[m], fine_tab, base_halo[...] + prolong_halo(got), f_acc.at[m])
 
-    for k in range(1, slices):
-        @pl.when(p + k < slices)
+    @pl.when(sends_term)
+    def _():
+        term_copy(p, 1).wait_send()
+
+    for k in (2, 1):
+        @pl.when(chain_on[k - 1])
         def _():
-            term_copy(p, k).wait_send()
+            chain_copy(k).wait_send()
 
     @pl.when(p + 1 < slices)
     def _():
@@ -573,6 +615,9 @@
                 pltpu.SemaphoreType.DMA((slices,)),
                 pltpu.SemaphoreType.DMA((2,)),
                 pltpu.SemaphoreType.DMA((2,)),
+                pltpu.VMEM((2, coarse_rows // 2, wide), F32),
+                pltpu.SemaphoreType.DMA((2,)),
+                pltpu.SemaphoreType.DMA,
             ],
             compiler_params=pltpu.CompilerParams(
                 collective_id=0, has_side_effects=True, vmem_limit_bytes=VMEM_LIMIT

time: 65.1 us -> 63.8 us (0.980)
  Pallas kernels: 63.2 us -> 61.9 us
    pallas_call x1, Pallas kernels: 63.2 us -> 61.9 us  [shards(): pl.pallas_call(functools.partial(kernel, geometry, places), out_shape=jax...]
where the time goes in v4:
time: 63.8 us; the launch traced here: 63.7 us
  Pallas kernels  61.9 us (97%)
  local copies, waits for them, and re-layouts  1.74 us (3%)
    pallas_call x1, Pallas kernels, shards(): pl.pallas_call(functools.partial(kernel, geometry, places), out_shape=jax...  61.9 us
    unnamed x3, local copies, waits for them, and re-layouts  1.74 us

profile of v4, /device:TPU:5, one launch (start us, length us, event | category | flops | bytes accessed | tf_op | source)
XLA Modules:
  0.0 63.7 jit_solution(17469438862376193544)
XLA Ops:
  0.0 0.0 copy-start
  0.0 1.0 %copy-done = f32[1,3,1,16,16,128]{5,4,3,2,1,0:T(8,128)S(1)} copy-done((f32[1,3,1,16,16,128]{5,4,3,2,1,0:T(8,128)S(1)}, f32[1,3,1,16,16,128]{5,4,3,2,1,0:T(8,128)}, u32[]{:S(2)}) %copy-start) | copy-done | bytes 393240
  1.0 61.9 %shard_map.28 = f32[3,256,128]{2,1,0:T(8,128)S(1)} custom-call(f32[3,256,128]{2,1,0:T(8,128)S(1)} %bitcast.5, bf16[8384,768]{1,0:T(8,128)(2,1)} %constant.2.clone.refs_0_), custom_call_target="tpu_custom_call" | custom-call | tf_op jit(solution)/shard_map/pallas_call | solution.py:586
  63.0 0.7 %copy.5 = f32[1,3,1,16,16,128]{5,4,3,2,1,0:T(8,128)} copy(f32[1,3,1,16,16,128]{5,4,3,2,1,0:T(8,128)S(1)} %bitcast.4) | data formatting | bytes 786432
Async XLA Ops:
  0.0 1.0 %copy-start = (f32[1,3,1,16,16,128]{5,4,3,2,1,0:T(8,128)S(1)}, f32[1,3,1,16,16,128]{5,4,3,2,1,0:T(8,128)}, u32[]{:S(2)}) copy-start(f32[1,3,1,16,16,128]{5,4,3,2,1,0:T(8,128)} %param.2) | copy-start | bytes 1179652

commit v5 on v4

--- a/solution.py
+++ b/solution.py
@@ -393,6 +393,10 @@
     def _():
         term_copy(p, 1).start()
 
+    @pl.when(p + 1 < slices)
+    def _():
+        hand_halo().start()
+
     @pl.when(odd == 1)
     def _():
         term_copy(p - 1, 1).wait_recv()
@@ -470,10 +474,6 @@
 
     lax.fori_loop(jnp.maximum(2 * chip - 1, 0), 2 * p, stage, 0)
     value = open_stage(2 * p)
-
-    @pl.when(p + 1 < slices)
-    def _():
-        hand_halo().start()
 
     @pl.when(p == 0)
     def _():

time: 63.8 us -> 63.8 us (level)
  no operation moved by 1% of the time
where the time goes in v5:
time: 63.8 us; the launch traced here: 63.7 us
  Pallas kernels  61.9 us (97%)
  local copies, waits for them, and re-layouts  1.74 us (3%)
    pallas_call x1, Pallas kernels, shards(): pl.pallas_call(functools.partial(kernel, geometry, places), out_shape=jax...  61.9 us
    unnamed x3, local copies, waits for them, and re-layouts  1.74 us

profile of v5, /device:TPU:5, one launch (start us, length us, event | category | flops | bytes accessed | tf_op | source)
XLA Modules:
  0.0 63.7 jit_solution(4919834277210329404)
XLA Ops:
  0.0 0.0 copy-start
  0.0 1.0 %copy-done = f32[1,3,1,16,16,128]{5,4,3,2,1,0:T(8,128)S(1)} copy-done((f32[1,3,1,16,16,128]{5,4,3,2,1,0:T(8,128)S(1)}, f32[1,3,1,16,16,128]{5,4,3,2,1,0:T(8,128)}, u32[]{:S(2)}) %copy-start) | copy-done | bytes 393240
  1.0 61.9 %shard_map.28 = f32[3,256,128]{2,1,0:T(8,128)S(1)} custom-call(f32[3,256,128]{2,1,0:T(8,128)S(1)} %bitcast.5, bf16[8384,768]{1,0:T(8,128)(2,1)} %constant.2.clone.refs_0_), custom_call_target="tpu_custom_call" | custom-call | tf_op jit(solution)/shard_map/pallas_call | solution.py:586
  62.9 0.7 %copy.5 = f32[1,3,1,16,16,128]{5,4,3,2,1,0:T(8,128)} copy(f32[1,3,1,16,16,128]{5,4,3,2,1,0:T(8,128)S(1)} %bitcast.4) | data formatting | bytes 786432
Async XLA Ops:
  0.0 1.0 %copy-start = (f32[1,3,1,16,16,128]{5,4,3,2,1,0:T(8,128)S(1)}, f32[1,3,1,16,16,128]{5,4,3,2,1,0:T(8,128)}, u32[]{:S(2)}) copy-start(f32[1,3,1,16,16,128]{5,4,3,2,1,0:T(8,128)} %param.2) | copy-start | bytes 1179652
